TPU v7x, 32 devices: a whole 2x2x4 slice. The times are simulated.
32 devices in a mesh: tm: 2 (over y), gx: 4 (over z), gy: 4 (over x, core).
Axes of the slice: x: 2, y: 2, z: 4, core: 2. Of those that a mesh axis runs over, the one named last changes fastest.
Arguments:
- provisional: float32 [2, 3, 3, 16, 64, 1024], P('tm', None, None, None, 'gx', 'gy'), may hold values from -1.5 to 1.5
Outputs:
- corrected: float32 [2, 3, 3, 16, 64, 1024], P('tm', None, None, None, 'gx', 'gy')
All inputs are finite; a program needn't handle non-finite values.
Results may differ from a plain program's by a relative error of at most 0.00002.
Values sent between devices are 32-bit elements; how exact they have to be, the bound alone decides.
A program may use at most 64 MiB of HBM per device.

v0:
```python
import functools

import jax
import jax.numpy as jnp
from jax import lax
from jax.experimental import pallas as pl
from jax.experimental.pallas import tpu as pltpu
from jax.sharding import PartitionSpec as P

viscosity = 0.1
slice_step = 0.25
half_step = 0.125
first_row = (5.0 / 24.0, 1.0 / 3.0, -1.0 / 24.0)
second_row = (-1.0 / 24.0, 1.0 / 3.0, 5.0 / 24.0)
q1 = tuple(slice_step * w for w in first_row)
q2 = tuple(slice_step * w for w in second_row)
LANES = 128


def kernel(
    n_tm, n_gx, n_gy, in_ref, out_ref,
    up, v1p, v2p, c0p, c1p, w0p, w1p, f0, s2, qa, qb, m1, m2,
    eu_s, eu_r, ev1_s, ev1_r, ev2_s, ev2_r, ew0_s, ew0_r, ew1_s, ew1_r,
    d_s, d_r, w_s, w_r,
    load_sem, send_sem, recv_sem, tm_send, tm_recv,
):
    _, _, X, Z, Y = in_ref.shape
    H = X // 2
    t, gx, gy = lax.axis_index("tm"), lax.axis_index("gx"), lax.axis_index("gy")
    has = {
        ("gx", 1): gx < n_gx - 1, ("gx", -1): gx > 0,
        ("gy", 1): gy < n_gy - 1, ("gy", -1): gy > 0,
        ("tm", 1): t < n_tm - 1, ("tm", -1): t > 0,
    }
    place = {"gx": gx, "gy": gy, "tm": t}

    def target(axis, step):
        size = {"gx": n_gx, "gy": n_gy, "tm": n_tm}[axis]
        moved = dict(place)
        moved[axis] = lax.rem(place[axis] + step + size, size)
        return (moved["tm"], moved["gx"], moved["gy"])

    load = pltpu.make_async_copy(in_ref, up.at[:, :, pl.ds(1, X)], load_sem)
    load.start()

    barrier = pltpu.get_barrier_semaphore()
    for (axis, step), there in has.items():
        @pl.when(there)
        def _(axis=axis, step=step):
            pl.semaphore_signal(
                barrier, inc=1, device_id=target(axis, step),
                device_id_type=pl.DeviceIdType.MESH,
            )
    peers = sum(jnp.where(there, 1, 0) for there in has.values())
    pl.semaphore_wait(barrier, peers)

    lane = lax.broadcasted_iota(jnp.int32, (Z, Y), 1)
    even = lane % 2 == 0
    elane = lax.broadcasted_iota(jnp.int32, (Z, LANES), 1)
    epair = elane // 2

    def remote(src, dst, p, d, axis, step):
        return pltpu.make_async_remote_copy(
            src_ref=src, dst_ref=dst, send_sem=send_sem.at[p, d], recv_sem=recv_sem.at[p, d],
            device_id=target(axis, step), device_id_type=pl.DeviceIdType.MESH,
        )

    def row(ref, i):
        return ref.at[:, :, pl.ds(i, 1)] if len(ref.shape) == 5 else ref.at[:, pl.ds(i, 1)]

    def rows_of(p, src, first, last, dst):
        return [
            (("gx", 1), remote(row(src, last), row(dst, 0), p, 0, "gx", 1)),
            (("gx", -1), remote(row(src, first), row(dst, X + 1), p, 1, "gx", -1)),
        ]

    def columns_of(p, es, er):
        return [
            (("gy", 1), remote(es.at[1], er.at[0], p, 2, "gy", 1)),
            (("gy", -1), remote(es.at[0], er.at[1], p, 3, "gy", -1)),
        ]

    def start(copies):
        for key, copy in copies:
            pl.when(has[key])(copy.start)

    def arrive(copies):
        for (axis, step), copy in copies:
            pl.when(has[(axis, -step)])(copy.wait_recv)

    def sent(copies):
        for key, copy in copies:
            pl.when(has[key])(copy.wait_send)

    def no_rows(dst):
        for key, i in ((("gx", -1), 0), (("gx", 1), X + 1)):
            @pl.when(jnp.logical_not(has[key]))
            def _(i=i):
                where_ = row(dst, i)
                where_[...] = jnp.zeros(where_.shape, jnp.float32)

    def no_columns(er):
        for key, i in ((("gy", -1), 0), (("gy", 1), 1)):
            @pl.when(jnp.logical_not(has[key]))
            def _(i=i):
                er[i] = jnp.zeros(er.shape[1:], jnp.float32)

    def G(get, x, low, high, k):
        mid = [get(c, x + 1) for c in range(3)]
        a = [0.5 * mid[0], (0.5 / k) * mid[1], 0.5 * mid[2]]
        nu = [viscosity, viscosity / (k * k), viscosity]
        ahead = [nu[i] - a[i] for i in range(3)]
        behind = [nu[i] + a[i] for i in range(3)]
        result = []
        for c in range(3):
            u = mid[c]
            at = c * X + x
            if k == 1:
                h = pltpu.roll(high, LANES - 1 - at, 1)
                l = pltpu.roll(low, lax.rem(LANES - at, LANES), 1)
            else:
                h = pltpu.roll(high, LANES - 2 - 2 * at, 1)
                l = pltpu.roll(low, lax.rem(LANES - 2 * at, LANES), 1)
            wide = Y // LANES
            north = jnp.where(lane >= Y - k, jnp.concatenate([h] * wide, 1), pltpu.roll(u, Y - k, 1))
            south = jnp.where(lane < k, jnp.concatenate([l] * wide, 1), pltpu.roll(u, k, 1))
            result.append(
                (ahead[0] * get(c, x + 2) + behind[0] * get(c, x))
                + (ahead[1] * north + behind[1] * south)
                + (ahead[2] * pltpu.roll(u, Z - 1, 0) + behind[2] * pltpu.roll(u, 1, 0))
                - (2.0 * sum(nu)) * u
            )
        return result

    def R(u):
        return 0.5 * (u + jnp.where(even, pltpu.roll(u, Y - 1, 1), pltpu.roll(u, 1, 1)))

    def put(acc, column, at, k):
        return jnp.where((elane if k == 1 else epair) == at, column, acc)

    def put_both(pair, u, at, k):
        return (put(pair[0], u[:, :1], at, k), put(pair[1], u[:, Y - 1:], at, k))

    blank = jnp.zeros((Z, LANES), jnp.float32)
    blanks = (blank, blank)

    def loop(body, carry, count=X):
        return lax.fori_loop(0, count, body, carry)

    u_rows = rows_of(0, in_ref, 0, X - 1, up)
    start(u_rows)
    no_rows(up)
    no_columns(eu_r)
    load.wait()

    def pack_u(x, carry):
        nodes, coarse = list(carry[:3]), carry[3]
        for c in range(3):
            at = c * X + x
            for n in range(3):
                nodes[n] = put_both(nodes[n], up[n, c, x + 1], at, 1)
            coarse = put_both(coarse, R(up[0, c, x + 1]), at, 2)
        return (*nodes, coarse)

    packed = loop(pack_u, (blanks,) * 4)
    for n in range(4):
        for side in range(2):
            eu_s[side, n] = packed[n][side]
    u_columns = columns_of(0, eu_s, eu_r)
    start(u_columns)
    arrive(u_rows)
    arrive(u_columns)

    def sweep_first(x, carry):
        fine, coarse = carry
        fluxes = [
            G(lambda c, i, n=n: up[n, c, i], x, eu_r[0, n], eu_r[1, n], 1) for n in range(3)
        ]
        for c in range(3):
            a, b, d = (fluxes[n][c] for n in range(3))
            v1 = up[0, c, x + 1] + (q1[0] * a + q1[1] * b + q1[2] * d)
            v1p[c, x + 1] = v1
            f0[c, x] = a
            s2[c, x] = q2[0] * a + (q2[1] - half_step) * b + q2[2] * d
            at = c * X + x
            fine = put_both(fine, v1, at, 1)
            coarse = put_both(coarse, R(v1), at, 2)
        return fine, coarse

    fine, coarse = loop(sweep_first, (blanks, blanks))
    for side in range(2):
        ev1_s[side, 0] = fine[side]
        ev1_s[side, 1] = coarse[side]
    v1_copies = rows_of(1, v1p, 1, X, v1p) + columns_of(1, ev1_s, ev1_r)
    start(v1_copies)
    no_rows(v1p)
    no_columns(ev1_r)

    def restrict_start(i, _):
        for c in range(3):
            c0p[c, i] = R(up[0, c, i])
        return 0

    loop(restrict_start, 0, X + 2)

    @pl.when(has[("tm", -1)])
    def _():
        def base_start(x, _):
            b0 = G(lambda c, i: c0p[c, i], x, eu_r[0, 3], eu_r[1, 3], 2)
            for c in range(3):
                m1[c, x] = -half_step * b0[c]
            return 0

        loop(base_start, 0)

    arrive(v1_copies)

    def sweep_second(x, fine):
        h1 = G(lambda c, i: v1p[c, i], x, ev1_r[0, 0], ev1_r[1, 0], 1)
        for c in range(3):
            v2 = v1p[c, x + 1] + half_step * h1[c] + s2[c, x]
            v2p[c, x + 1] = v2
            a = f0[c, x]
            qa[c, x] = q1[0] * a + q1[1] * h1[c]
            qb[c, x] = q2[0] * a + q2[1] * h1[c]
            fine = put_both(fine, v2, c * X + x, 1)
        return fine

    fine = loop(sweep_second, blanks)
    for side in range(2):
        ev2_s[side, 0] = fine[side]
    v2_copies = rows_of(2, v2p, 1, X, v2p) + columns_of(2, ev2_s, ev2_r)
    start(v2_copies)
    no_rows(v2p)
    no_columns(ev2_r)

    def detail(x, _):
        for c in range(3):
            a, b = v2p[c, x + 1], v2p[c, x + H + 1]
            d_s[c, x] = jnp.where(even, a - R(a), b - R(b))
        return 0

    def along(src, dst, p):
        return pltpu.make_async_remote_copy(
            src_ref=src, dst_ref=dst, send_sem=tm_send.at[p], recv_sem=tm_recv.at[p],
            device_id=target("tm", 1), device_id_type=pl.DeviceIdType.MESH,
        )

    d_copy = [(("tm", 1), along(d_s, d_r, 0))]
    w_copy = [(("tm", 1), along(w_s, w_r, 1))]

    @pl.when(has[("tm", 1)])
    def _():
        loop(detail, 0, H)

    start(d_copy)

    def restrict_middle(i, _):
        for c in range(3):
            c1p[c, i] = R(v1p[c, i])
        return 0

    loop(restrict_middle, 0, X + 2)

    def base_middle(x, _):
        b1 = G(lambda c, i: c1p[c, i], x, ev1_r[0, 1], ev1_r[1, 1], 2)
        for c in range(3):
            m2[c, x] = -half_step * b1[c]
        return 0

    loop(base_middle, 0)
    arrive(v2_copies)

    leader = t == 0

    def sweep_third(x, coarse):
        h2 = G(lambda c, i: v2p[c, i], x, ev2_r[0, 0], ev2_r[1, 0], 1)
        for c in range(3):
            a1 = R(qa[c, x] + q1[2] * h2[c])
            a2 = R(qb[c, x] + q2[2] * h2[c])
            m2[c, x] = m2[c, x] + a2
            w1 = c0p[c, x + 1] + a1
            w1p[c, x + 1] = w1
            qa[c, x] = a1
            coarse = put_both(coarse, w1, c * X + x, 2)
        return coarse

    coarse = loop(sweep_third, blanks)

    w0_copies = rows_of(3, w0p, 1, X, w0p) + columns_of(3, ew0_s, ew0_r)
    w1_copies = rows_of(4, w1p, 1, X, w1p) + columns_of(4, ew1_s, ew1_r)

    @pl.when(leader)
    def _():
        for side in range(2):
            ew1_s[side, 0] = coarse[side]

    @pl.when(has[("tm", -1)])
    def _():
        arrive(w_copy)

        def unpack(x, coarse):
            for c in range(3):
                w = w_r[c, x]
                a = jnp.where(even, w, pltpu.roll(w, 1, 1))
                b = jnp.where(even, pltpu.roll(w, Y - 1, 1), w)
                w0p[c, x + 1] = a
                w0p[c, x + H + 1] = b
                coarse = put_both(coarse, a, c * X + x, 2)
                coarse = put_both(coarse, b, c * X + x + H, 2)
            return coarse

        coarse = loop(unpack, blanks, H)
        for side in range(2):
            ew0_s[side, 0] = coarse[side]
        start(w0_copies)
        no_rows(w0p)
        no_columns(ew0_r)
        arrive(w0_copies)

        def chain_middle(x, coarse):
            g = G(lambda c, i: w0p[c, i], x, ew0_r[0, 0], ew0_r[1, 0], 2)
            for c in range(3):
                w1 = w0p[c, x + 1] + half_step * g[c] + (m1[c, x] + qa[c, x])
                w1p[c, x + 1] = w1
                coarse = put_both(coarse, w1, c * X + x, 2)
            return coarse

        coarse = loop(chain_middle, blanks)
        for side in range(2):
            ew1_s[side, 0] = coarse[side]

    start(w1_copies)
    no_rows(w1p)
    no_columns(ew1_r)

    def middle_out(x, _):
        for c in range(3):
            out_ref[1, c, x] = v1p[c, x + 1] + (w1p[c, x + 1] - c1p[c, x + 1])
        return 0

    loop(middle_out, 0)

    @pl.when(leader)
    def _():
        def start_out(x, _):
            for c in range(3):
                out_ref[0, c, x] = up[0, c, x + 1]
            return 0

        loop(start_out, 0)

    arrive(w1_copies)

    def chain_final(x, _):
        low, high = ew1_r[0, 0], ew1_r[1, 0]
        ga = G(lambda c, i: w1p[c, i], x, low, high, 2)
        gb = G(lambda c, i: w1p[c, i], x + H, low, high, 2)
        for c in range(3):
            ends = []
            for g, i in ((ga, x), (gb, x + H)):
                w2 = w1p[c, i + 1] + half_step * g[c] + m2[c, i]
                v2 = v2p[c, i + 1]
                out_ref[2, c, i] = v2 + (w2 - R(v2))
                ends.append(w2)
            w_s[c, x] = jnp.where(even, ends[0], ends[1])
        return 0

    loop(chain_final, 0, H)
    start(w_copy)

    @pl.when(has[("tm", -1)])
    def _():
        arrive(d_copy)

        def start_out(x, _):
            for c in range(3):
                d = d_r[c, x]
                a = jnp.where(even, d, -pltpu.roll(d, 1, 1))
                b = jnp.where(even, -pltpu.roll(d, Y - 1, 1), d)
                out_ref[0, c, x] = w0p[c, x + 1] + a
                out_ref[0, c, x + H] = w0p[c, x + H + 1] + b
            return 0

        loop(start_out, 0, H)
        sent(w0_copies)

    for copies in (u_rows, u_columns, v1_copies, v2_copies, w1_copies, d_copy, w_copy):
        sent(copies)


def per_device(sizes, provisional):
    block = jnp.swapaxes(provisional[0], 2, 3)
    _, _, X, Z, Y = block.shape
    f32 = jnp.float32
    padded = pltpu.VMEM((3, X + 2, Z, Y), f32)
    plain = pltpu.VMEM((3, X, Z, Y), f32)
    half = pltpu.VMEM((3, X // 2, Z, Y), f32)

    def edges(count):
        return [pltpu.VMEM((2, count, Z, LANES), f32)] * 2

    out = pl.pallas_call(
        functools.partial(kernel, *sizes),
        out_shape=jax.ShapeDtypeStruct(block.shape, f32),
        in_specs=[pl.BlockSpec(memory_space=pl.ANY)],
        out_specs=pl.BlockSpec(memory_space=pltpu.VMEM),
        scratch_shapes=[
            pltpu.VMEM((3, 3, X + 2, Z, Y), f32),
            *[padded] * 6,
            *[plain] * 6,
            *edges(4), *edges(2), *edges(1), *edges(1), *edges(1),
            *[half] * 4,
            pltpu.SemaphoreType.DMA,
            pltpu.SemaphoreType.DMA((5, 4)),
            pltpu.SemaphoreType.DMA((5, 4)),
            pltpu.SemaphoreType.DMA((2,)),
            pltpu.SemaphoreType.DMA((2,)),
        ],
        compiler_params=pltpu.CompilerParams(
            collective_id=0, has_side_effects=True, vmem_limit_bytes=40 * 1024 * 1024
        ),
    )(block)
    return jnp.swapaxes(out, 2, 3)[None]


def solution(mesh):
    sizes = tuple(mesh.shape[axis] for axis in ("tm", "gx", "gy"))
    spec = P("tm", None, None, None, "gx", "gy")
    return jax.shard_map(
        functools.partial(per_device, sizes), mesh=mesh, in_specs=(spec,), out_specs=spec,
        check_vma=False,
    )
```

profile of v0, /device:TPU:4, one launch (start us, length us, event | category | flops | bytes accessed | tf_op | source)
XLA Modules:
  0.0 63.1 jit_solution(3660871810210854720)
XLA Ops:
  0.0 3.0 %copy.5 = f32[1,3,3,16,16,256]{5,3,4,2,1,0:T(8,128)S(1)} copy(f32[1,3,3,16,16,256]{5,4,3,2,1,0:T(8,128)} %param.1) | data formatting | bytes 4718592 | tf_op args[0]
  3.1 57.3 %shard_map.17 = f32[3,3,16,16,256]{4,3,2,1,0:T(8,128)S(1)} custom-call(f32[3,3,16,16,256]{4,3,2,1,0:T(8,128)S(1)} %bitcast.9), custom_call_target="tpu_custom_call" | custom-call | tf_op jit(solution)/shard_map/pallas_call | solution.py:403
  60.4 2.8 %copy.3 = f32[1,3,3,16,16,256]{5,4,3,2,1,0:T(8,128)} copy(f32[1,3,3,16,16,256]{5,3,4,2,1,0:T(8,128)S(1)} %bitcast.8) | data formatting | bytes 4718592 | tf_op jit(solution)/shard_map/broadcast_in_dim | solution.py:424
where the time goes:
time: 63.3 us; the launch traced here: 63.1 us
  Pallas kernels  57.3 us (91%)
  local copies, waits for them, and re-layouts  5.82 us (9%)
    pallas_call x1, Pallas kernels, per_device(): pl.pallas_call(functools.partial(kernel, *sizes), out_shape=jax.ShapeDtyp...  57.3 us
    unnamed x1, local copies, waits for them, and re-layouts  3.05 us
    broadcast_in_dim x1, local copies, waits for them, and re-layouts, per_device(): return jnp.swapaxes(out, 2, 3)[None]  2.77 us

commit v1 on v0

--- a/solution.py
+++ b/solution.py
@@ -19,7 +19,7 @@
 
 def kernel(
     n_tm, n_gx, n_gy, in_ref, out_ref,
-    up, v1p, v2p, c0p, c1p, w0p, w1p, f0, s2, qa, qb, m1, m2,
+    up, v1p, v2p, c0p, c1p, w0p, w1p, w2p, f0, s2, qa, qb, m1, m2,
     eu_s, eu_r, ev1_s, ev1_r, ev2_s, ev2_r, ew0_s, ew0_r, ew1_s, ew1_r,
     d_s, d_r, w_s, w_r,
     load_sem, send_sem, recv_sem, tm_send, tm_recv,
@@ -32,23 +32,29 @@
         ("gy", 1): gy < n_gy - 1, ("gy", -1): gy > 0,
         ("tm", 1): t < n_tm - 1, ("tm", -1): t > 0,
     }
+    for axis in ("gx", "gy"):
+        for step in (1, -1):
+            for slice_ in (1, -1):
+                has[(axis, step, slice_)] = jnp.logical_and(has[(axis, step)], has[("tm", slice_)])
     place = {"gx": gx, "gy": gy, "tm": t}
 
-    def target(axis, step):
-        size = {"gx": n_gx, "gy": n_gy, "tm": n_tm}[axis]
+    def target(axis, step, slice_=0):
+        size = {"gx": n_gx, "gy": n_gy, "tm": n_tm}
         moved = dict(place)
-        moved[axis] = lax.rem(place[axis] + step + size, size)
+        moved[axis] = lax.rem(place[axis] + step + size[axis], size[axis])
+        if slice_ != 0:
+            moved["tm"] = lax.rem(t + slice_ + n_tm, n_tm)
         return (moved["tm"], moved["gx"], moved["gy"])
 
     load = pltpu.make_async_copy(in_ref, up.at[:, :, pl.ds(1, X)], load_sem)
     load.start()
 
     barrier = pltpu.get_barrier_semaphore()
-    for (axis, step), there in has.items():
+    for peer, there in has.items():
         @pl.when(there)
-        def _(axis=axis, step=step):
+        def _(peer=peer):
             pl.semaphore_signal(
-                barrier, inc=1, device_id=target(axis, step),
+                barrier, inc=1, device_id=target(*peer),
                 device_id_type=pl.DeviceIdType.MESH,
             )
     peers = sum(jnp.where(there, 1, 0) for there in has.values())
@@ -59,10 +65,10 @@
     elane = lax.broadcasted_iota(jnp.int32, (Z, LANES), 1)
     epair = elane // 2
 
-    def remote(src, dst, p, d, axis, step):
+    def remote(src, dst, p, d, axis, step, slice_=0):
         return pltpu.make_async_remote_copy(
             src_ref=src, dst_ref=dst, send_sem=send_sem.at[p, d], recv_sem=recv_sem.at[p, d],
-            device_id=target(axis, step), device_id_type=pl.DeviceIdType.MESH,
+            device_id=target(axis, step, slice_), device_id_type=pl.DeviceIdType.MESH,
         )
 
     def row(ref, i):
@@ -85,8 +91,8 @@
             pl.when(has[key])(copy.start)
 
     def arrive(copies):
-        for (axis, step), copy in copies:
-            pl.when(has[(axis, -step)])(copy.wait_recv)
+        for (axis, *steps), copy in copies:
+            pl.when(has[(axis, *[-step for step in steps])])(copy.wait_recv)
 
     def sent(copies):
         for key, copy in copies:
@@ -144,8 +150,13 @@
     blank = jnp.zeros((Z, LANES), jnp.float32)
     blanks = (blank, blank)
 
-    def loop(body, carry, count=X):
-        return lax.fori_loop(0, count, body, carry)
+    def loop(body, carry, count=X, first=0):
+        return lax.fori_loop(first, count, body, carry)
+
+    def edges_first(body, carry, copies):
+        carry = loop(lambda i, carry: body(i * (X - 1), carry), carry, 2)
+        start(copies)
+        return loop(body, carry, X - 1, 1)
 
     u_rows = rows_of(0, in_ref, 0, X - 1, up)
     start(u_rows)
@@ -187,12 +198,14 @@
             coarse = put_both(coarse, R(v1), at, 2)
         return fine, coarse
 
-    fine, coarse = loop(sweep_first, (blanks, blanks))
+    v1_rows = rows_of(1, v1p, 1, X, v1p)
+    v1_columns = columns_of(1, ev1_s, ev1_r)
+    v1_copies = v1_rows + v1_columns
+    fine, coarse = edges_first(sweep_first, (blanks, blanks), v1_rows)
     for side in range(2):
         ev1_s[side, 0] = fine[side]
         ev1_s[side, 1] = coarse[side]
-    v1_copies = rows_of(1, v1p, 1, X, v1p) + columns_of(1, ev1_s, ev1_r)
-    start(v1_copies)
+    start(v1_columns)
     no_rows(v1p)
     no_columns(ev1_r)
 
@@ -226,11 +239,13 @@
             fine = put_both(fine, v2, c * X + x, 1)
         return fine
 
-    fine = loop(sweep_second, blanks)
+    v2_rows = rows_of(2, v2p, 1, X, v2p)
+    v2_columns = columns_of(2, ev2_s, ev2_r)
+    v2_copies = v2_rows + v2_columns
+    fine = edges_first(sweep_second, blanks, v2_rows)
     for side in range(2):
         ev2_s[side, 0] = fine[side]
-    v2_copies = rows_of(2, v2p, 1, X, v2p) + columns_of(2, ev2_s, ev2_r)
-    start(v2_copies)
+    start(v2_columns)
     no_rows(v2p)
     no_columns(ev2_r)
 
@@ -247,7 +262,21 @@
         )
 
     d_copy = [(("tm", 1), along(d_s, d_r, 0))]
-    w_copy = [(("tm", 1), along(w_s, w_r, 1))]
+    spans = [(0, 1), (H - 1, 1)]
+    spans += [(i, min(2, H - 1 - i)) for i in range(1, H - 1, 2)]
+    spans = spans[: max(1, H)]
+    w_parts = [
+        [(("tm", 1), along(w_s.at[:, pl.ds(i, n)], w_r.at[:, pl.ds(i, n)], 1 + j))]
+        for j, (i, n) in enumerate(spans)
+    ]
+    w0_rows = [
+        (("gx", 1, 1), remote(row(w2p, X - 1), row(w0p, 0), 3, 0, "gx", 1, 1)),
+        (("gx", -1, 1), remote(row(w2p, 0), row(w0p, X + 1), 3, 1, "gx", -1, 1)),
+    ]
+    w0_columns = [
+        (("gy", 1, 1), remote(ew0_s.at[1], ew0_r.at[0], 3, 2, "gy", 1, 1)),
+        (("gy", -1, 1), remote(ew0_s.at[0], ew0_r.at[1], 3, 3, "gy", -1, 1)),
+    ]
 
     @pl.when(has[("tm", 1)])
     def _():
@@ -279,58 +308,56 @@
             a1 = R(qa[c, x] + q1[2] * h2[c])
             a2 = R(qb[c, x] + q2[2] * h2[c])
             m2[c, x] = m2[c, x] + a2
-            w1 = c0p[c, x + 1] + a1
-            w1p[c, x + 1] = w1
-            qa[c, x] = a1
-            coarse = put_both(coarse, w1, c * X + x, 2)
+            if coarse is None:
+                m1[c, x] = m1[c, x] + a1
+            else:
+                w1 = c0p[c, x + 1] + a1
+                w1p[c, x + 1] = w1
+                coarse = put_both(coarse, w1, c * X + x, 2)
         return coarse
 
-    coarse = loop(sweep_third, blanks)
-
-    w0_copies = rows_of(3, w0p, 1, X, w0p) + columns_of(3, ew0_s, ew0_r)
-    w1_copies = rows_of(4, w1p, 1, X, w1p) + columns_of(4, ew1_s, ew1_r)
+    w1_rows = rows_of(4, w1p, 1, X, w1p)
+    w1_columns = columns_of(4, ew1_s, ew1_r)
+    w1_copies = w1_rows + w1_columns
 
     @pl.when(leader)
     def _():
+        coarse = edges_first(sweep_third, blanks, w1_rows)
         for side in range(2):
             ew1_s[side, 0] = coarse[side]
 
     @pl.when(has[("tm", -1)])
     def _():
-        arrive(w_copy)
-
-        def unpack(x, coarse):
-            for c in range(3):
-                w = w_r[c, x]
-                a = jnp.where(even, w, pltpu.roll(w, 1, 1))
-                b = jnp.where(even, pltpu.roll(w, Y - 1, 1), w)
-                w0p[c, x + 1] = a
-                w0p[c, x + H + 1] = b
-                coarse = put_both(coarse, a, c * X + x, 2)
-                coarse = put_both(coarse, b, c * X + x + H, 2)
-            return coarse
-
-        coarse = loop(unpack, blanks, H)
-        for side in range(2):
-            ew0_s[side, 0] = coarse[side]
-        start(w0_copies)
+        loop(lambda x, _: sweep_third(x, None) or 0, 0)
         no_rows(w0p)
         no_columns(ew0_r)
-        arrive(w0_copies)
+
+        def unpack(x, _):
+            for c in range(3):
+                w = w_r[c, x]
+                w0p[c, x + 1] = jnp.where(even, w, pltpu.roll(w, 1, 1))
+                w0p[c, x + H + 1] = jnp.where(even, pltpu.roll(w, Y - 1, 1), w)
+            return 0
+
+        for part, (i, n) in zip(w_parts, spans):
+            arrive(part)
+            loop(unpack, 0, i + n, i)
+        arrive(w0_rows)
+        arrive(w0_columns)
 
         def chain_middle(x, coarse):
             g = G(lambda c, i: w0p[c, i], x, ew0_r[0, 0], ew0_r[1, 0], 2)
             for c in range(3):
-                w1 = w0p[c, x + 1] + half_step * g[c] + (m1[c, x] + qa[c, x])
+                w1 = w0p[c, x + 1] + half_step * g[c] + m1[c, x]
                 w1p[c, x + 1] = w1
                 coarse = put_both(coarse, w1, c * X + x, 2)
             return coarse
 
-        coarse = loop(chain_middle, blanks)
+        coarse = edges_first(chain_middle, blanks, w1_rows)
         for side in range(2):
             ew1_s[side, 0] = coarse[side]
 
-    start(w1_copies)
+    start(w1_columns)
     no_rows(w1p)
     no_columns(ew1_r)
 
@@ -349,25 +376,6 @@
             return 0
 
         loop(start_out, 0)
-
-    arrive(w1_copies)
-
-    def chain_final(x, _):
-        low, high = ew1_r[0, 0], ew1_r[1, 0]
-        ga = G(lambda c, i: w1p[c, i], x, low, high, 2)
-        gb = G(lambda c, i: w1p[c, i], x + H, low, high, 2)
-        for c in range(3):
-            ends = []
-            for g, i in ((ga, x), (gb, x + H)):
-                w2 = w1p[c, i + 1] + half_step * g[c] + m2[c, i]
-                v2 = v2p[c, i + 1]
-                out_ref[2, c, i] = v2 + (w2 - R(v2))
-                ends.append(w2)
-            w_s[c, x] = jnp.where(even, ends[0], ends[1])
-        return 0
-
-    loop(chain_final, 0, H)
-    start(w_copy)
 
     @pl.when(has[("tm", -1)])
     def _():
@@ -383,9 +391,56 @@
             return 0
 
         loop(start_out, 0, H)
-        sent(w0_copies)
-
-    for copies in (u_rows, u_columns, v1_copies, v2_copies, w1_copies, d_copy, w_copy):
+
+    arrive(w1_copies)
+
+    def chain_end(x):
+        g = G(lambda c, i: w1p[c, i], x, ew1_r[0, 0], ew1_r[1, 0], 2)
+        return [w1p[c, x + 1] + half_step * g[c] + m2[c, x] for c in range(3)]
+
+    def end_out(c, x, w2):
+        v2 = v2p[c, x + 1]
+        out_ref[2, c, x] = v2 + (w2 - R(v2))
+
+    @pl.when(has[("tm", 1)])
+    def _():
+        def pair(x, coarse):
+            ends = (chain_end(x), chain_end(x + H))
+            for c in range(3):
+                w_s[c, x] = jnp.where(even, ends[0][c], ends[1][c])
+                for end, i in zip(ends, (x, x + H)):
+                    w2p[c, i] = end[c]
+                    coarse = put_both(coarse, end[c], c * X + i, 2)
+            return coarse
+
+        coarse = blanks
+        for j, (part, (i, n)) in enumerate(zip(w_parts, spans)):
+            coarse = loop(pair, coarse, i + n, i)
+            start(part)
+            if j == min(1, len(spans) - 1):
+                start(w0_rows)
+        for side in range(2):
+            ew0_s[side, 0] = coarse[side]
+        start(w0_columns)
+
+        def passed_out(x, _):
+            for c in range(3):
+                end_out(c, x, w2p[c, x])
+            return 0
+
+        loop(passed_out, 0)
+
+    @pl.when(jnp.logical_not(has[("tm", 1)]))
+    def _():
+        def last_out(x, _):
+            w2 = chain_end(x)
+            for c in range(3):
+                end_out(c, x, w2[c])
+            return 0
+
+        loop(last_out, 0)
+
+    for copies in (u_rows, u_columns, v1_copies, v2_copies, w1_copies, d_copy, *w_parts, w0_rows, w0_columns):
         sent(copies)
 
 
@@ -408,14 +463,14 @@
         scratch_shapes=[
             pltpu.VMEM((3, 3, X + 2, Z, Y), f32),
             *[padded] * 6,
-            *[plain] * 6,
+            *[plain] * 7,
             *edges(4), *edges(2), *edges(1), *edges(1), *edges(1),
             *[half] * 4,
             pltpu.SemaphoreType.DMA,
             pltpu.SemaphoreType.DMA((5, 4)),
             pltpu.SemaphoreType.DMA((5, 4)),
-            pltpu.SemaphoreType.DMA((2,)),
-            pltpu.SemaphoreType.DMA((2,)),
+            pltpu.SemaphoreType.DMA((X,)),
+            pltpu.SemaphoreType.DMA((X,)),
         ],
         compiler_params=pltpu.CompilerParams(
             collective_id=0, has_side_effects=True, vmem_limit_bytes=40 * 1024 * 1024

time: 63.3 us -> 56.9 us (0.90)
  the two profiles are of different devices: /device:TPU:4 before, /device:TPU:13 now
where the time goes in v1:
time: 56.9 us; the launch traced here: 56.8 us
  Pallas kernels  51 us (90%)
  local copies, waits for them, and re-layouts  5.82 us (10%)
    pallas_call x1, Pallas kernels, per_device(): pl.pallas_call(functools.partial(kernel, *sizes), out_shape=jax.ShapeDtyp...  51 us
    unnamed x1, local copies, waits for them, and re-layouts  3.05 us
    broadcast_in_dim x1, local copies, waits for them, and re-layouts, per_device(): return jnp.swapaxes(out, 2, 3)[None]  2.77 us

profile of v1, /device:TPU:13, one launch (start us, length us, event | category | flops | bytes accessed | tf_op | source)
XLA Modules:
  0.0 56.8 jit_solution(5540703254316824757)
XLA Ops:
  0.0 3.0 %copy.5 = f32[1,3,3,16,16,256]{5,3,4,2,1,0:T(8,128)S(1)} copy(f32[1,3,3,16,16,256]{5,4,3,2,1,0:T(8,128)} %param.1) | data formatting | bytes 4718592 | tf_op args[0]
  3.1 51.0 %shard_map.17 = f32[3,3,16,16,256]{4,3,2,1,0:T(8,128)S(1)} custom-call(f32[3,3,16,16,256]{4,3,2,1,0:T(8,128)S(1)} %bitcast.9), custom_call_target="tpu_custom_call" | custom-call | tf_op jit(solution)/shard_map/pallas_call | solution.py:458
  54.0 2.8 %copy.3 = f32[1,3,3,16,16,256]{5,4,3,2,1,0:T(8,128)} copy(f32[1,3,3,16,16,256]{5,3,4,2,1,0:T(8,128)S(1)} %bitcast.8) | data formatting | bytes 4718592 | tf_op jit(solution)/shard_map/broadcast_in_dim | solution.py:479

commit v2 on v1

--- a/solution.py
+++ b/solution.py
@@ -151,7 +151,7 @@
     blanks = (blank, blank)
 
     def loop(body, carry, count=X, first=0):
-        return lax.fori_loop(first, count, body, carry)
+        return lax.fori_loop(first, count, body, carry, unroll=2 if (count - first) % 2 == 0 else 1)
 
     def edges_first(body, carry, copies):
         carry = loop(lambda i, carry: body(i * (X - 1), carry), carry, 2)

time: 56.9 us -> 52.8 us (0.928)
  Pallas kernels: 51 us -> 46.8 us
    pallas_call x1, Pallas kernels: 51 us -> 46.8 us  [per_device(): pl.pallas_call(functools.partial(kernel, *sizes), out_shape=jax.ShapeDtyp...]
where the time goes in v2:
time: 52.8 us; the launch traced here: 52.7 us
  Pallas kernels  46.8 us (89%)
  local copies, waits for them, and re-layouts  5.82 us (11%)
    pallas_call x1, Pallas kernels, per_device(): pl.pallas_call(functools.partial(kernel, *sizes), out_shape=jax.ShapeDtyp...  46.8 us
    unnamed x1, local copies, waits for them, and re-layouts  3.05 us
    broadcast_in_dim x1, local copies, waits for them, and re-layouts, per_device(): return jnp.swapaxes(out, 2, 3)[None]  2.77 us

profile of v2, /device:TPU:13, one launch (start us, length us, event | category | flops | bytes accessed | tf_op | source)
XLA Modules:
  0.0 52.7 jit_solution(8650275451933387369)
XLA Ops:
  0.0 3.0 %copy.5 = f32[1,3,3,16,16,256]{5,3,4,2,1,0:T(8,128)S(1)} copy(f32[1,3,3,16,16,256]{5,4,3,2,1,0:T(8,128)} %param.1) | data formatting | bytes 4718592 | tf_op args[0]
  3.1 46.8 %shard_map.17 = f32[3,3,16,16,256]{4,3,2,1,0:T(8,128)S(1)} custom-call(f32[3,3,16,16,256]{4,3,2,1,0:T(8,128)S(1)} %bitcast.9), custom_call_target="tpu_custom_call" | custom-call | tf_op jit(solution)/shard_map/pallas_call | solution.py:458
  49.9 2.8 %copy.3 = f32[1,3,3,16,16,256]{5,4,3,2,1,0:T(8,128)} copy(f32[1,3,3,16,16,256]{5,3,4,2,1,0:T(8,128)S(1)} %bitcast.8) | data formatting | bytes 4718592 | tf_op jit(solution)/shard_map/broadcast_in_dim | solution.py:479
